TPU v7x, 32 devices: a whole 2x2x4 slice. The times are simulated.
32 devices in a mesh: slab: 8 (over z, y), term: 4 (over x, core).
Axes of the slice: x: 2, y: 2, z: 4, core: 2. Of those that a mesh axis runs over, the one named last changes fastest.
Arguments:
- right_side: float32 [84, 16, 128, 128], P('term', 'slab'), may hold values from -24 to 24
- mean_cond: float32 [16, 128, 128], P('slab', 'term'), may hold values from 2 to 4
- cond_terms: float32 [6, 16, 128, 128], P(None, 'slab', 'term'), may hold values from -0.3 to 0.3
Outputs:
- solution: float32 [84, 16, 128, 128], P('term', 'slab')
- residual: float32 [84, 16, 128, 128], P('term', 'slab')
All inputs are finite; a program needn't handle non-finite values.
Results may differ from a plain program's by a relative error of at most 0.00013.
Values sent between devices are 32-bit elements; how exact they have to be, the bound alone decides.
A program may use at most 64 MiB of HBM per device.

v0:
```python
import math

import jax
import jax.numpy as jnp
from jax import lax
from jax.sharding import PartitionSpec as P

DIM = 6
DEG = 3
ITERS = 2


lower_edge = 2.0
upper_edge = 72.0


def extended_2(array, sides, width):
    for axis, dim in sides:
        devices, length = (lax.axis_size(axis), array.shape[dim])
        up = [(i, (i + 1) % devices) for i in range(devices - 1)]
        down = [(j, i) for i, j in up]
        last = lax.slice_in_dim(array, length - width, length, axis=dim)
        leading = lax.slice_in_dim(array, 0, width, axis=dim)
        before = lax.ppermute(last, axis, up)
        after = lax.ppermute(leading, axis, down)
        array = jnp.concatenate([before, array, after], axis=dim)
    return array


def compositions(degree_sum, slots_left):
    if slots_left == 1:
        return [[degree_sum]]
    listing = []
    for leading in range(degree_sum, -1, -1):
        for remainder in compositions(degree_sum - leading, slots_left - 1):
            listing.append([leading] + remainder)
    return listing


def galerkin_tables(variables, degree):
    indices = []
    for degree_level in range(degree + 1):
        indices.extend(compositions(degree_level, variables))
    count = len(indices)
    tables = []
    for variable in range(variables):
        rows_list = []
        for row in range(count):
            first = indices[row]
            entries = []
            for col in range(count):
                second = indices[col]
                agreeing = all((first[m] == second[m] for m in range(variables) if m != variable))
                value = 0.0
                if agreeing and abs(first[variable] - second[variable]) == 1:
                    higher = max(first[variable], second[variable])
                    value = higher / math.sqrt(4.0 * higher * higher - 1.0)
                entries.append(value)
            rows_list.append(entries)
        tables.append(rows_list)
    return tables


def laplace(extended, field):
    beside = extended[:, 2:, 1:-1, 1:-1] + extended[:, :-2, 1:-1, 1:-1]
    beside = beside + extended[:, 1:-1, 2:, 1:-1] + extended[:, 1:-1, :-2, 1:-1]
    beside = beside + extended[:, 1:-1, 1:-1, 2:] + extended[:, 1:-1, 1:-1, :-2]
    return 6.0 * field - beside


def coupling(lap_field, mean_cond, cond_terms, tables):
    flat = lap_field.reshape(lap_field.shape[0], -1)
    result = mean_cond.reshape(1, -1) * flat
    terms_flat = cond_terms.reshape(cond_terms.shape[0], -1)
    for variable in range(cond_terms.shape[0]):
        mixed = jnp.dot(
            tables[variable],
            flat,
            precision=lax.Precision.HIGHEST,
            preferred_element_type=jnp.float32,
        )
        result = result + terms_flat[variable][None, :] * mixed
    return result.reshape(lap_field.shape)


def chebyshev(right_side, apply_operator):
    center_value = 0.5 * (upper_edge + lower_edge)
    half_width = 0.5 * (upper_edge - lower_edge)
    sigma_value = center_value / half_width
    rho_now = 1.0 / sigma_value
    residual = right_side
    direction = right_side / center_value
    solution = jnp.zeros_like(right_side)
    for iteration in range(ITERS):
        solution = solution + direction
        residual = residual - apply_operator(direction)
        rho_next = 1.0 / (2.0 * sigma_value - rho_now)
        if iteration + 1 < ITERS:
            direction = rho_next * rho_now * direction + 2.0 * rho_next / half_width * residual
        rho_now = rho_next
    return (solution, residual)


def shards(right_side, mean_cond, cond_terms):
    tables = jnp.asarray(galerkin_tables(DIM, DEG), jnp.float32)

    def apply_operator(field):
        extended = extended_2(field, (("slab", 1),), 1)
        extended = jnp.pad(extended, ((0, 0), (0, 0), (1, 1), (1, 1)))
        lap_field = laplace(extended, field)
        banded = lax.all_to_all(lap_field, "term", split_axis=2, concat_axis=0, tiled=True)
        mixed = coupling(banded, mean_cond, cond_terms, tables)
        return lax.all_to_all(mixed, "term", split_axis=0, concat_axis=2, tiled=True)

    solution, residual = chebyshev(right_side, apply_operator)
    return (solution, residual)


def solution(mesh):
    placed = (P("term", "slab", None, None), P("slab", "term", None), P(None, "slab", "term", None))
    return jax.shard_map(
        shards,
        mesh=mesh,
        in_specs=placed,
        out_specs=(P("term", "slab", None, None), P("term", "slab", None, None)),
        check_vma=False,
    )
```

profile of v0, /device:TPU:0, one launch (start us, length us, event | category | flops | bytes accessed | tf_op | source)
XLA Modules:
  0.0 362.3 jit_solution(15543242781081698601)
XLA Ops:
  2.9 5.0 %collective-permute-start.1 = (f32[21,1,128,128]{3,2,1,0:T(8,128)S(1)}, f32[21,1,128,128]{3,2,1,0:T(8,128)S(1)}, u32[]{:S(2)}, u32[]{:S(2)}) collective-permute-start(f32[21,1,128,128]{3,2,1,0:T(8,128)S(1)} %get-tuple-element.8), channel_id=1, source_target_pairs={{0,4},{4,8},{8,12},{12,16},{16,20},{20,24},{24,28},{1,5},{5,9},{9,... | collective-permute-start | bytes 4128776 | tf_op jit(solution)/shard_map/ppermute | solution.py:24
  9.4 57.3 %collective-permute-done.1 = f32[21,1,128,128]{3,2,1,0:T(8,128)S(1)} collective-permute-done((f32[21,1,128,128]{3,2,1,0:T(8,128)S(1)}, f32[21,1,128,128]{3,2,1,0:T(8,128)S(1)}, u32[]{:S(2)}, u32[]{:S(2)}) %collective-permute-start.1) | collective-permute-done | bytes 1376288 | tf_op jit(solution)/shard_map/ppermute | solution.py:24
  67.8 4.8 %select_maximum_fusion.2 = f32[21,4,130,130]{3,2,1,0:T(8,128)S(1)} fusion(f32[21,1,128,128]{3,2,1,0:T(8,128)S(1)} %collective-permute-done, f32[21,2,128,128]{3,2,1,0:T(8,128)S(1)} %broadcast_multiply_fusion, f32[21,1,128,128]{3,2,1,0:T(8,128)S(1)} %collective-permute-done.1), kind=kLoop, calls=%fused_computation.6 | loop fusion | flops 21294000 | bytes 11183424 | tf_op jit(solution)/shard_map/concatenate | solution.py:26
  72.6 3.7 %fusion.29 = f32[21,2,128,128]{3,2,1,0:T(8,128)S(1)} fusion(f32[21,4,130,130]{3,2,1,0:T(8,128)S(1)} %select_maximum_fusion.2, f32[21,2,128,128]{3,2,1,0:T(8,128)S(1)} %broadcast_multiply_fusion, f32[21,1,128,128]{3,2,1,0:T(8,128)S(1)} %collective-permute-done.1, f32[21,1,128,128]{3,2,1,0:T(8,128)} %copy-done.5, f32[21,2,128,128]{3,2,1,0:T(8,128)S(1)} %copy-done), kind=kLoop, calls=%fused_computation.56 | loop fusion | flops 6193152 | bytes 22020096 | tf_op jit(solution)/shard_map/sub | solution.py:68
  76.3 3.3 copy.20
  79.5 3.8 %all-to-all-start = ((f32[21,2,128,128]{3,0,1,2:T(8,128)}), f32[21,2,128,128]{3,0,1,2:T(8,128)S(1)}, u32[]{:S(2)}, u32[]{:S(2)}) async-start(f32[21,2,128,128]{3,0,1,2:T(8,128)} %copy.20), calls=%async_computation | async-start | bytes 6291456 | tf_op jit(solution)/shard_map/all_to_all | solution.py:111
  83.4 36.9 %all-to-all-done = f32[21,2,128,128]{3,0,1,2:T(8,128)S(1)} async-done(((f32[21,2,128,128]{3,0,1,2:T(8,128)}), f32[21,2,128,128]{3,0,1,2:T(8,128)S(1)}, u32[]{:S(2)}, u32[]{:S(2)}) %all-to-all-start) | async-done | bytes 2752544 | tf_op jit(solution)/shard_map/all_to_all | solution.py:111
  120.3 2.4 copy.31
  122.6 2.9 reshape.35
  125.6 3.2 fusion.26
  128.8 3.1 fusion.24
  132.0 3.1 fusion.22
  135.1 3.1 fusion.20
  138.3 3.5 fusion.18
  141.8 3.1 fusion.16
  145.8 35.2 %all_to_all.66 = f32[84,2,32,128]{3,2,1,0:T(8,128)S(1)} all-to-all(f32[84,2,32,128]{3,2,1,0:T(8,128)S(1)} %bitcast.121), channel_id=1, replica_groups=mesh['slab'=8,'term'=4] {'term'}, dimensions={0} | all-to-all | bytes 5505024 | tf_op jit(solution)/shard_map/all_to_all | solution.py:113
  182.8 2.4 fusion.31
  185.4 4.5 %collective-permute-start.3 = (f32[21,1,128,128]{3,2,1,0:T(8,128)S(1)}, f32[21,1,128,128]{3,2,1,0:T(8,128)S(1)}, u32[]{:S(2)}, u32[]{:S(2)}) collective-permute-start(f32[21,1,128,128]{3,2,1,0:T(8,128)S(1)} %get-tuple-element.6), channel_id=1, source_target_pairs={{0,4},{4,8},{8,12},{12,16},{16,20},{20,24},{24,28},{1,5},{5,9},{9,... | collective-permute-start | bytes 4128776 | tf_op jit(solution)/shard_map/ppermute | solution.py:24
  191.2 57.2 %collective-permute-done.3 = f32[21,1,128,128]{3,2,1,0:T(8,128)S(1)} collective-permute-done((f32[21,1,128,128]{3,2,1,0:T(8,128)S(1)}, f32[21,1,128,128]{3,2,1,0:T(8,128)S(1)}, u32[]{:S(2)}, u32[]{:S(2)}) %collective-permute-start.3) | collective-permute-done | bytes 1376288 | tf_op jit(solution)/shard_map/ppermute | solution.py:24
  248.4 4.8 %select_maximum_fusion = f32[21,4,130,130]{3,2,1,0:T(8,128)S(1)} fusion(f32[21,1,128,128]{3,2,1,0:T(8,128)S(1)} %collective-permute-done.2, f32[21,2,128,128]{3,2,1,0:T(8,128)S(1)} %get-tuple-element.5, f32[21,1,128,128]{3,2,1,0:T(8,128)S(1)} %collective-permute-done.3), kind=kLoop, calls=%fused_computation.4 | loop fusion | flops 21294000 | bytes 11183424 | tf_op jit(solution)/shard_map/concatenate | solution.py:26
  253.1 2.6 fusion.27
  257.4 39.4 %all_to_all.67 = f32[21,2,128,128]{3,0,1,2:T(8,128)S(1)} all-to-all(f32[21,2,128,128]{3,0,1,2:T(8,128)S(1)} %copy.23), channel_id=1, replica_groups=mesh['slab'=8,'term'=4] {'term'}, dimensions={2} | all-to-all | bytes 5505024 | tf_op jit(solution)/shard_map/all_to_all | solution.py:111
  296.8 2.4 copy.30
  299.2 2.9 reshape.37
  302.1 3.2 fusion.14
  305.3 3.1 fusion.12
  308.4 3.1 fusion.10
  311.6 3.1 fusion.8
  314.7 3.4 fusion.6
  318.0 3.1 fusion.4
  321.9 35.2 %all_to_all.68 = f32[84,2,32,128]{3,2,1,0:T(8,128)S(1)} all-to-all(f32[84,2,32,128]{3,2,1,0:T(8,128)S(1)} %bitcast.124), channel_id=1, replica_groups=mesh['slab'=8,'term'=4] {'term'}, dimensions={0} | all-to-all | bytes 5505024 | tf_op jit(solution)/shard_map/all_to_all | solution.py:113
  359.7 2.3 bitcast_subtract_fusion
  (43 shorter events, 14.0 us)
Async XLA Ops:
  2.9 63.8 %collective-permute-start.1 = (f32[21,1,128,128]{3,2,1,0:T(8,128)S(1)}, f32[21,1,128,128]{3,2,1,0:T(8,128)S(1)}, u32[]{:S(2)}, u32[]{:S(2)}) collective-permute-start(f32[21,1,128,128]{3,2,1,0:T(8,128)S(1)} %get-tuple-element.8), channel_id=1, source_target_pairs={{0,4},{4,8},{8,12},{12,16},{16,20},{20,24},{24,28},{1,5},{5,9},{9,... | collective-permute-start | bytes 4128776 | tf_op jit(solution)/shard_map/ppermute | solution.py:24
  7.9 64.7 %copy-start = (f32[21,2,128,128]{3,2,1,0:T(8,128)S(1)}, f32[21,2,128,128]{3,2,1,0:T(8,128)}, u32[]{:S(2)}) copy-start(f32[21,2,128,128]{3,2,1,0:T(8,128)} %param.4) | copy-start | bytes 8257540
  7.9 58.8 %collective-permute-start = (f32[21,1,128,128]{3,2,1,0:T(8,128)S(1)}, f32[21,1,128,128]{3,2,1,0:T(8,128)S(1)}, u32[]{:S(2)}, u32[]{:S(2)}) collective-permute-start(f32[21,1,128,128]{3,2,1,0:T(8,128)S(1)} %get-tuple-element.9), channel_id=1, source_target_pairs={{4,0},{8,4},{12,8},{16,12},{20,16},{24,20},{28,24},{5,1},{9,5},{13... | collective-permute-start | bytes 4128776 | tf_op jit(solution)/shard_map/ppermute | solution.py:25
  66.7 1.1 copy-start.5
  79.5 3.8 %copy-start.6 = (f32[6,2,32,128]{3,2,1,0:T(8,128)S(1)}, f32[6,2,32,128]{3,2,1,0:T(8,128)}, u32[]{:S(2)}) copy-start(f32[6,2,32,128]{3,2,1,0:T(8,128)} %param.6) | copy-start | bytes 589828
  79.5 40.7 %all-to-all-start = ((f32[21,2,128,128]{3,0,1,2:T(8,128)}), f32[21,2,128,128]{3,0,1,2:T(8,128)S(1)}, u32[]{:S(2)}, u32[]{:S(2)}) async-start(f32[21,2,128,128]{3,0,1,2:T(8,128)} %copy.20), calls=%async_computation | async-start | bytes 6291456 | tf_op jit(solution)/shard_map/all_to_all | solution.py:111
  122.6 2.9 copy-start.11
  122.6 2.9 copy-start.13
  125.6 3.2 copy-start.12
  128.8 3.2 copy-start.10
  131.9 3.1 copy-start.9
  135.1 3.1 copy-start.8
  138.3 3.6 copy-start.7
  181.0 1.8 copy-start.1
  182.8 2.4 copy-start.3
  185.4 62.9 %collective-permute-start.3 = (f32[21,1,128,128]{3,2,1,0:T(8,128)S(1)}, f32[21,1,128,128]{3,2,1,0:T(8,128)S(1)}, u32[]{:S(2)}, u32[]{:S(2)}) collective-permute-start(f32[21,1,128,128]{3,2,1,0:T(8,128)S(1)} %get-tuple-element.6), channel_id=1, source_target_pairs={{0,4},{4,8},{8,12},{12,16},{16,20},{20,24},{24,28},{1,5},{5,9},{9,... | collective-permute-start | bytes 4128776 | tf_op jit(solution)/shard_map/ppermute | solution.py:24
  189.9 58.5 %collective-permute-start.2 = (f32[21,1,128,128]{3,2,1,0:T(8,128)S(1)}, f32[21,1,128,128]{3,2,1,0:T(8,128)S(1)}, u32[]{:S(2)}, u32[]{:S(2)}) collective-permute-start(f32[21,1,128,128]{3,2,1,0:T(8,128)S(1)} %get-tuple-element.7), channel_id=1, source_target_pairs={{4,0},{8,4},{12,8},{16,12},{20,16},{24,20},{28,24},{5,1},{9,5},{13... | collective-permute-start | bytes 4128776 | tf_op jit(solution)/shard_map/ppermute | solution.py:25
  357.1 1.8 copy-start.2
  357.1 2.6 copy-start.4
where the time goes:
time: 369 us; the launch traced here: 362 us
  waiting for transfers between devices  151 us (41%)
  blocking collectives  110 us (30%)
  matrix products  38.3 us (10%)
  local copies, waits for them, and re-layouts  22.9 us (6%)
  other arithmetic  22.6 us (6%)
  starting transfers between devices  16.1 us (4%)
    ppermute x2, waiting for transfers between devices, extended_2(): before = lax.ppermute(last, axis, up)  114 us
    all_to_all x2, blocking collectives, apply_operator(): lax.all_to_all(mixed, 'term', split_axis=0, concat_axis=2, tiled=True)  70.4 us
    all_to_all x1, blocking collectives, apply_operator(): lax.all_to_all(lap_field, 'term', split_axis=2, concat_axis=0, tiled=True)  39.4 us
    dot_general x12, matrix products, coupling(): jnp.dot(tables[variable], flat, precision=lax.Precision.HIGHEST, preferre...  38.3 us
    all_to_all x1, waiting for transfers between devices, apply_operator(): lax.all_to_all(lap_field, 'term', split_axis=2, concat_axis=0, tiled=True)  36.9 us
    concatenate x2, other arithmetic, extended_2(): array = jnp.concatenate([before, array, after], axis=dim)  9.51 us
    ppermute x2, starting transfers between devices, extended_2(): before = lax.ppermute(last, axis, up)  9.43 us
  transfers between devices with their start and end apart: 5, of which 3 were waited for; matrix products, arithmetic and copies ran while one was open for 0% of the time, Pallas kernels for 0%

commit v1 on v0

v1 whole, which is shorter than its diff:
```python
import functools
import math

import jax
import jax.numpy as jnp
from jax import lax
from jax.experimental import pallas as pl
from jax.experimental.pallas import tpu as pltpu
from jax.sharding import PartitionSpec as P

DIM = 6
DEG = 3
ITERS = 2

lower_edge = 2.0
upper_edge = 72.0


def compositions(degree_sum, slots_left):
    if slots_left == 1:
        return [[degree_sum]]
    listing = []
    for leading in range(degree_sum, -1, -1):
        for remainder in compositions(degree_sum - leading, slots_left - 1):
            listing.append([leading] + remainder)
    return listing


def galerkin_entries(variables, degree):
    indices = []
    for degree_level in range(degree + 1):
        indices.extend(tuple(c) for c in compositions(degree_level, variables))
    place = {index: i for i, index in enumerate(indices)}
    rows = []
    for index in indices:
        per_variable = []
        for variable in range(variables):
            entries = []
            for step in (-1, 1):
                other = list(index)
                other[variable] += step
                col = place.get(tuple(other))
                if col is not None:
                    higher = max(index[variable], other[variable])
                    entries.append((col, higher / math.sqrt(4.0 * higher * higher - 1.0)))
            per_variable.append(entries)
        rows.append(per_variable)
    return rows


def kernel(
    dims,
    b_hbm, mean_hbm, cond_hbm,
    sol_hbm, res_hbm,
    bufb, bufd, lap, r1, sol, cond,
    rows_out, rows_in,
    local_sem, b_send, b_recv, c_send, c_recv, z_send, z_recv, r_send, r_recv, o_send, o_recv,
):
    slabs, nt, tp, zp, rb, terms = dims
    planes = 2 * zp
    pairs = slabs // 2
    bands = 2 * nt
    first, last = 8, 8 + rb
    s = lax.axis_index("slab")
    t = lax.axis_index("term")
    q = s // 2
    h = s % 2
    g = 2 * t + (h + t) % 2

    def band_of(hh, tt):
        return 2 * tt + (hh + tt) % 2

    def owner(band):
        tt = band // 2
        return (band % 2 + tt) % 2, tt

    def dev(qq, hh, tt):
        return {"slab": 2 * qq + hh, "term": tt}

    offsets = [(dh, dt) for dh in range(2) for dt in range(nt) if (dh, dt) != (0, 0)]

    def partner(sign, dh, dt):
        return (h + dh) % 2, (t + sign * dt + nt) % nt

    barrier = pltpu.get_barrier_semaphore()
    for dh, dt in offsets:
        hh, tt = partner(1, dh, dt)
        pl.semaphore_signal(barrier, inc=1, device_id=dev(q, hh, tt), device_id_type=pl.DeviceIdType.MESH)

    @pl.when(q > 0)
    def _():
        pl.semaphore_signal(barrier, inc=1, device_id=dev(q - 1, h, t), device_id_type=pl.DeviceIdType.MESH)

    @pl.when(q < pairs - 1)
    def _():
        pl.semaphore_signal(barrier, inc=1, device_id=dev(q + 1, h, t), device_id_type=pl.DeviceIdType.MESH)

    below = (q + pairs - 1) // pairs
    above = (2 * pairs - 2 - q) // pairs
    pl.semaphore_wait(barrier, len(offsets) + below + above)

    def remote(src, dst, send, recv, device):
        return pltpu.make_async_remote_copy(
            src_ref=src, dst_ref=dst, send_sem=send, recv_sem=recv,
            device_id=device, device_id_type=pl.DeviceIdType.MESH,
        )

    def band_rows(band):
        return pl.ds(pl.multiple_of(band * rb, 8), rb)

    own_dst = bufb.at[pl.ds(t * tp, tp), pl.ds(1 + h * zp, zp), pl.ds(first, rb), :]
    b_copies = []
    for n, (dh, dt) in enumerate(offsets):
        hh, tt = partner(1, dh, dt)
        copy = remote(
            b_hbm.at[:, :, band_rows(band_of(hh, tt)), :], own_dst,
            b_send.at[n], b_recv.at[n], dev(q, hh, tt),
        )
        copy.start()
        b_copies.append(copy)
    own_b = pltpu.make_async_copy(b_hbm.at[:, :, band_rows(g), :], own_dst, local_sem.at[0])
    own_b.start()

    def half(hh):
        return pl.ds(pl.multiple_of(rb * ((hh + t) % 2), 8), rb)

    my_planes = pl.ds(h * zp, zp)
    other = dev(q, 1 - h, t)
    c_copies = [
        remote(cond_hbm.at[:, :, half(1 - h), :], cond.at[pl.ds(0, DIM), my_planes], c_send.at[0], c_recv.at[0], other),
        remote(mean_hbm.at[:, half(1 - h), :], cond.at[DIM, my_planes], c_send.at[1], c_recv.at[1], other),
    ]
    own_c = [
        pltpu.make_async_copy(cond_hbm.at[:, :, half(h), :], cond.at[pl.ds(0, DIM), my_planes], local_sem.at[1]),
        pltpu.make_async_copy(mean_hbm.at[:, half(h), :], cond.at[DIM, my_planes], local_sem.at[2]),
    ]
    for copy in c_copies + own_c:
        copy.start()

    def clear(plane):
        def body(j, carry):
            zero = jnp.zeros((rb, 128), jnp.float32)
            bufb[j, plane, first:last, :] = zero
            bufd[j, plane, first:last, :] = zero
            return carry
        lax.fori_loop(0, terms, body, 0)

    @pl.when(q == 0)
    def _():
        clear(0)

    @pl.when(q == pairs - 1)
    def _():
        clear(planes + 1)

    @pl.when(g == 0)
    def _():
        rows_in[0, 0] = jnp.zeros(rows_in.shape[2:], jnp.float32)
        rows_in[1, 0] = jnp.zeros(rows_in.shape[2:], jnp.float32)

    @pl.when(g == bands - 1)
    def _():
        rows_in[0, 1] = jnp.zeros(rows_in.shape[2:], jnp.float32)
        rows_in[1, 1] = jnp.zeros(rows_in.shape[2:], jnp.float32)

    def z_copy(step, buf, hh, part, at, size):
        slot = step * bands + hh * nt + part
        return remote(
            buf.at[pl.ds(at, size), 1 + (planes - 1) * hh, pl.ds(first, rb), :],
            buf.at[pl.ds(at, size), (planes + 1) * (1 - hh), pl.ds(first, rb), :],
            z_send.at[slot], z_recv.at[slot], dev(q - 1 + 2 * hh, h, t),
        )

    def z_sends(hh):
        target = q - 1 + 2 * hh
        return jnp.logical_and(target >= 0, target < pairs)

    def z_receives(hh):
        source = q + 1 - 2 * hh
        return jnp.logical_and(source >= 0, source < pairs)

    def forward(hh, tt):
        @pl.when(z_sends(hh))
        def _():
            z_copy(0, bufb, hh, tt, tt * tp, tp).start()

    own_b.wait()
    forward(h, t)
    for n, (dh, dt) in enumerate(offsets):
        b_copies[n].wait_recv()
        hh, tt = partner(-1, dh, dt)
        forward(hh, tt)

    def row_copies(step):
        up_h, up_t = owner(lax.rem(g + bands - 1, bands))
        down_h, down_t = owner(lax.rem(g + 1, bands))
        up = remote(rows_out.at[step, 0], rows_in.at[step, 1], r_send.at[step, 0], r_recv.at[step, 1], dev(q, up_h, up_t))
        down = remote(rows_out.at[step, 1], rows_in.at[step, 0], r_send.at[step, 1], r_recv.at[step, 0], dev(q, down_h, down_t))
        return up, down

    def pack(step, buf):
        def body(jj, carry):
            for a in range(2):
                for p in range(planes):
                    at = planes * a + p
                    rows_out[step, 0, jj, at:at + 1, :] = buf[2 * jj + a, p + 1, first:first + 1, :]
                    rows_out[step, 1, jj, at:at + 1, :] = buf[2 * jj + a, p + 1, last - 1:last, :]
            return carry
        lax.fori_loop(0, terms // 2, body, 0)

    def start_rows(step):
        up, down = row_copies(step)

        @pl.when(g > 0)
        def _():
            up.start()

        @pl.when(g < bands - 1)
        def _():
            down.start()

    def wait_rows(step):
        up, down = row_copies(step)

        @pl.when(g > 0)
        def _():
            down.wait_recv()
            up.wait_send()

        @pl.when(g < bands - 1)
        def _():
            up.wait_recv()
            down.wait_send()

    def laplacian(step, buf):
        lane = lax.broadcasted_iota(jnp.int32, (planes, rb, 128), 2)
        inner = slice(1, planes + 1)

        def body(jj, carry):
            for a in range(2):
                j = 2 * jj + a
                for p in range(planes):
                    at = planes * a + p
                    buf[j, p + 1, first - 1:first, :] = rows_in[step, 0, jj, at:at + 1, :]
                    buf[j, p + 1, last:last + 1, :] = rows_in[step, 1, jj, at:at + 1, :]
            for a in range(2):
                j = 2 * jj + a
                field = buf[j, inner, first:last, :]
                beside = buf[j, 2:planes + 2, first:last, :] + buf[j, 0:planes, first:last, :]
                beside = beside + buf[j, inner, first + 1:last + 1, :] + buf[j, inner, first - 1:last - 1, :]
                after = jnp.where(lane == 127, 0.0, pltpu.roll(field, 127, 2))
                before = jnp.where(lane == 0, 0.0, pltpu.roll(field, 1, 2))
                lap[j] = 6.0 * field - (beside + after + before)
            return carry
        lax.fori_loop(0, terms // 2, body, 0)

    table = galerkin_entries(DIM, DEG)

    def coupled(finish):
        def body(p, carry):
            factors = [cond[k, p] for k in range(DIM)]
            mean = cond[DIM, p]
            for i in range(terms):
                total = mean * lap[i, p]
                for k in range(DIM):
                    mixed = None
                    for col, value in table[i][k]:
                        part = value * lap[col, p]
                        mixed = part if mixed is None else mixed + part
                    if mixed is not None:
                        total = total + factors[k] * mixed
                finish(i, p, total)
            return carry
        lax.fori_loop(0, planes, body, 0)

    center = 0.5 * (upper_edge + lower_edge)
    half_width = 0.5 * (upper_edge - lower_edge)
    sigma = center / half_width
    rho = 1.0 / sigma
    rho_next = 1.0 / (2.0 * sigma - rho)

    def finish_first(i, p, total):
        b = bufb[i, p + 1, first:last, :]
        residual = b - (1.0 / center) * total
        start = (1.0 / center) * b
        direction = (rho_next * rho) * start + (2.0 * rho_next / half_width) * residual
        r1[i, p] = residual
        bufd[i, p + 1, first:last, :] = direction
        sol[i, p] = start + direction

    def finish_second(i, p, total):
        r1[i, p] = r1[i, p] - total

    def out_copies(which, src, dst):
        copies = []
        for n, (dh, dt) in enumerate(offsets):
            hh, tt = partner(1, dh, dt)
            slot = which * len(offsets) + n
            copies.append(remote(
                src.at[pl.ds(tt * tp, tp), pl.ds(hh * zp, zp)],
                dst.at[:, :, band_rows(g), :],
                o_send.at[slot], o_recv.at[slot], dev(q, hh, tt),
            ))
        own = pltpu.make_async_copy(
            src.at[pl.ds(t * tp, tp), pl.ds(h * zp, zp)], dst.at[:, :, band_rows(g), :], local_sem.at[3 + which])
        return copies, own

    pack(0, bufb)
    start_rows(0)
    for copy in own_c:
        copy.wait()
    for copy in c_copies:
        copy.wait()
    for hh in range(2):
        for tt in range(nt):
            @pl.when(z_receives(hh))
            def _(hh=hh, tt=tt):
                z_copy(0, bufb, hh, tt, tt * tp, tp).wait_recv()
    wait_rows(0)
    laplacian(0, bufb)
    coupled(finish_first)

    pack(1, bufd)
    start_rows(1)
    for hh in range(2):
        @pl.when(z_sends(hh))
        def _(hh=hh):
            z_copy(1, bufd, hh, 0, 0, terms).start()
    sol_copies, sol_own = out_copies(0, sol, sol_hbm)
    for copy in sol_copies:
        copy.start()
    sol_own.start()
    for hh in range(2):
        @pl.when(z_receives(hh))
        def _(hh=hh):
            z_copy(1, bufd, hh, 0, 0, terms).wait_recv()
    wait_rows(1)
    laplacian(1, bufd)
    coupled(finish_second)
    res_copies, res_own = out_copies(1, r1, res_hbm)
    for copy in res_copies:
        copy.start()
    res_own.start()

    for copy in b_copies:
        copy.wait_send()
    for hh in range(2):
        @pl.when(z_sends(hh))
        def _(hh=hh):
            for tt in range(nt):
                z_copy(0, bufb, hh, tt, tt * tp, tp).wait_send()
            z_copy(1, bufd, hh, 0, 0, terms).wait_send()
    sol_own.wait()
    for copy in sol_copies:
        copy.wait()
    res_own.wait()
    for copy in res_copies:
        copy.wait()


def solution(mesh):
    slabs, nt = mesh.shape["slab"], mesh.shape["term"]

    def shards(right_side, mean_cond, cond_terms):
        tp, zp, ny, nx = right_side.shape
        terms = tp * nt
        rb = ny // (2 * nt)
        planes = 2 * zp
        partners = 2 * nt - 1
        dims = (slabs, nt, tp, zp, rb, terms)
        any_space = pl.BlockSpec(memory_space=pl.ANY)
        return pl.pallas_call(
            functools.partial(kernel, dims),
            out_shape=[jax.ShapeDtypeStruct(right_side.shape, jnp.float32)] * 2,
            in_specs=[any_space] * 3,
            out_specs=[any_space] * 2,
            scratch_shapes=[
                pltpu.VMEM((terms, planes + 2, rb + 16, nx), jnp.float32),
                pltpu.VMEM((terms, planes + 2, rb + 16, nx), jnp.float32),
                pltpu.VMEM((terms, planes, rb, nx), jnp.float32),
                pltpu.VMEM((terms, planes, rb, nx), jnp.float32),
                pltpu.VMEM((terms, planes, rb, nx), jnp.float32),
                pltpu.VMEM((DIM + 1, planes, rb, nx), jnp.float32),
                pltpu.VMEM((2, 2, terms // 2, 2 * planes, nx), jnp.float32),
                pltpu.VMEM((2, 2, terms // 2, 2 * planes, nx), jnp.float32),
                pltpu.SemaphoreType.DMA((5,)),
                pltpu.SemaphoreType.DMA((partners,)),
                pltpu.SemaphoreType.DMA((partners,)),
                pltpu.SemaphoreType.DMA((2,)),
                pltpu.SemaphoreType.DMA((2,)),
                pltpu.SemaphoreType.DMA((4 * nt,)),
                pltpu.SemaphoreType.DMA((4 * nt,)),
                pltpu.SemaphoreType.DMA((2, 2)),
                pltpu.SemaphoreType.DMA((2, 2)),
                pltpu.SemaphoreType.DMA((2 * partners,)),
                pltpu.SemaphoreType.DMA((2 * partners,)),
            ],
            compiler_params=pltpu.CompilerParams(
                collective_id=0, has_side_effects=True, vmem_limit_bytes=48 * 2**20
            ),
        )(right_side, mean_cond, cond_terms)

    placed = (P("term", "slab", None, None), P("slab", "term", None), P(None, "slab", "term", None))
    return jax.shard_map(
        shards,
        mesh=mesh,
        in_specs=placed,
        out_specs=(P("term", "slab", None, None), P("term", "slab", None, None)),
        check_vma=False,
    )
```

time: 369 us -> 120 us (0.33); the launches traced: 362 us -> 120 us
  waiting for transfers between devices: 151 us -> 0 us
  Pallas kernels: 0 us -> 115 us
  blocking collectives: 110 us -> 0 us
  matrix products: 38.3 us -> 0 us
  other arithmetic: 22.6 us -> 0 us
  local copies, waits for them, and re-layouts: 22.9 us -> 4.75 us
  starting transfers between devices: 16.1 us -> 0 us
    pallas_call x0 -> x1, Pallas kernels: none -> 115 us  [shards(): pl.pallas_call(functools.partial(kernel, dims), out_shape=[jax.ShapeDtype...]
    ppermute x4 -> x0, waiting for transfers between devices: 114 us -> none  [the longest x2 114 us: extended_2(): before = lax.ppermute(last, axis, up)]
    all_to_all x3 -> x0, blocking collectives: 110 us -> none  [the longest x2 70.4 us: apply_operator(): lax.all_to_all(mixed, 'term', split_axis=0, concat_axis=2, tiled=True)]
    dot_general x12 -> x0, matrix products: 38.3 us -> none  [coupling(): jnp.dot(tables[variable], flat, precision=lax.Precision.HIGHEST, preferre...]
    all_to_all x1 -> x0, waiting for transfers between devices: 36.9 us -> none  [apply_operator(): lax.all_to_all(lap_field, 'term', split_axis=2, concat_axis=0, tiled=True)]
    ppermute x4 -> x0, starting transfers between devices: 12.3 us -> none  [the longest x2 9.43 us: extended_2(): before = lax.ppermute(last, axis, up)]
    concatenate x2 -> x0, other arithmetic: 9.51 us -> none  [extended_2(): array = jnp.concatenate([before, array, after], axis=dim)]
    sub x3 -> x0, other arithmetic: 8.61 us -> none  [the longest x2 6.29 us: laplace(): return 6.0 * field - beside]
  transfers between devices with their start and end apart: 5 -> 0, of which waited for: 3 -> 0; matrix products, arithmetic and copies ran while one was open for 0% -> 0% of each run, Pallas kernels for 0% -> 0%
where the time goes in v1:
time: 120 us
  Pallas kernels  115 us (96%)
  local copies, waits for them, and re-layouts  4.75 us (4%)
    pallas_call x1, Pallas kernels, shards(): pl.pallas_call(functools.partial(kernel, dims), out_shape=[jax.ShapeDtype...  115 us
    unnamed x6, local copies, waits for them, and re-layouts  4.75 us

profile of v1, /device:TPU:0, one launch (start us, length us, event | category | flops | bytes accessed | tf_op | source)
XLA Modules:
  0.0 119.9 jit_solution(3873357825970604008)
XLA Ops:
  0.6 0.0 copy-start
  0.6 0.9 copy-done
  1.6 0.0 copy-start.1
  1.6 0.8 copy-done.1
  2.3 114.5 %shard_map.50 = (f32[21,2,128,128]{3,2,1,0:T(8,128)S(1)}, f32[21,2,128,128]{3,2,1,0:T(8,128)S(1)}) custom-call(f32[21,2,128,128]{3,2,1,0:T(8,128)} %b_hbm.1, f32[2,32,128]{2,1,0:T(8,128)S(1)} %copy-done.1, f32[6,2,32,128]{3,2,1,0:T(8,128)S(1)} %copy-done), custom_call_target="tpu_custom_call" | custom-call | tf_op jit(solution)/shard_map/pallas_call | solution.py:372
  116.9 1.5 %copy.7 = f32[21,2,128,128]{3,2,1,0:T(8,128)} copy(f32[21,2,128,128]{3,2,1,0:T(8,128)S(1)} %get-tuple-element.4) | data formatting | bytes 5505024
  118.4 1.5 %copy.8 = f32[21,2,128,128]{3,2,1,0:T(8,128)} copy(f32[21,2,128,128]{3,2,1,0:T(8,128)S(1)} %get-tuple-element.5) | data formatting | bytes 5505024
Async XLA Ops:
  0.6 0.9 copy-start
  1.6 0.8 copy-start.1

commit v2 on v1

v2 whole, which is shorter than its diff:
```python
import functools
import math

import jax
import jax.numpy as jnp
from jax import lax
from jax.experimental import pallas as pl
from jax.experimental.pallas import tpu as pltpu
from jax.sharding import PartitionSpec as P

DIM = 6
DEG = 3
ITERS = 2

lower_edge = 2.0
upper_edge = 72.0


def compositions(degree_sum, slots_left):
    if slots_left == 1:
        return [[degree_sum]]
    listing = []
    for leading in range(degree_sum, -1, -1):
        for remainder in compositions(degree_sum - leading, slots_left - 1):
            listing.append([leading] + remainder)
    return listing


def galerkin_entries(variables, degree):
    indices = []
    for degree_level in range(degree + 1):
        indices.extend(tuple(c) for c in compositions(degree_level, variables))
    place = {index: i for i, index in enumerate(indices)}
    rows = []
    for index in indices:
        per_variable = []
        for variable in range(variables):
            entries = []
            for step in (-1, 1):
                other = list(index)
                other[variable] += step
                col = place.get(tuple(other))
                if col is not None:
                    higher = max(index[variable], other[variable])
                    entries.append((col, higher / math.sqrt(4.0 * higher * higher - 1.0)))
            per_variable.append(entries)
        rows.append(per_variable)
    return rows


def kernel(
    dims,
    b_hbm, mean_hbm, cond_hbm,
    sol_hbm, res_hbm,
    bufb, bufd, lap, r1, sol, cond,
    rows_out, rows_in,
    local_sem, b_send, b_recv, c_send, c_recv, z_send, z_recv, r_send, r_recv, o_send, o_recv,
):
    slabs, nt, tp, rb, terms = dims
    pairs = slabs // 2
    bands = 2 * nt
    first, last = 8, 8 + rb
    s = lax.axis_index("slab")
    t = lax.axis_index("term")
    q = s // 2
    h = s % 2
    g = 2 * t + (h + t) % 2

    def band_of(hh, tt):
        return 2 * tt + (hh + tt) % 2

    def owner(band):
        tt = band // 2
        return (band % 2 + tt) % 2, tt

    def dev(qq, hh, tt):
        return {"slab": 2 * qq + hh, "term": tt}

    offsets = [(dh, dt) for dh in (1, 0) for dt in range(nt - 1, -1, -1) if (dh, dt) != (0, 0)]

    def partner(sign, dh, dt):
        return (h + dh) % 2, (t + sign * dt + nt) % nt

    barrier = pltpu.get_barrier_semaphore()
    for dh, dt in offsets:
        hh, tt = partner(1, dh, dt)
        pl.semaphore_signal(barrier, inc=1, device_id=dev(q, hh, tt), device_id_type=pl.DeviceIdType.MESH)

    @pl.when(q > 0)
    def _():
        pl.semaphore_signal(barrier, inc=1, device_id=dev(q - 1, h, t), device_id_type=pl.DeviceIdType.MESH)

    @pl.when(q < pairs - 1)
    def _():
        pl.semaphore_signal(barrier, inc=1, device_id=dev(q + 1, h, t), device_id_type=pl.DeviceIdType.MESH)

    below = (q + pairs - 1) // pairs
    above = (2 * pairs - 2 - q) // pairs
    pl.semaphore_wait(barrier, len(offsets) + below + above)

    def remote(src, dst, send, recv, device):
        return pltpu.make_async_remote_copy(
            src_ref=src, dst_ref=dst, send_sem=send, recv_sem=recv,
            device_id=device, device_id_type=pl.DeviceIdType.MESH,
        )

    def band_rows(band):
        return pl.ds(pl.multiple_of(band * rb, 8), rb)

    def b_pair(part, band):
        plane = h if part == 0 else 1 - h
        src = b_hbm.at[:, plane, band_rows(band), :]
        dst = bufb.at[pl.ds(t * tp, tp), 1 + 2 * h + plane, pl.ds(first, rb), :]
        return src, dst

    b_copies = []
    for part in range(2):
        for n, (dh, dt) in enumerate(offsets):
            hh, tt = partner(1, dh, dt)
            src, dst = b_pair(part, band_of(hh, tt))
            slot = part * len(offsets) + n
            copy = remote(src, dst, b_send.at[slot], b_recv.at[slot], dev(q, hh, tt))
            copy.start()
            b_copies.append(copy)
    own_b = [pltpu.make_async_copy(*b_pair(part, g), local_sem.at[part]) for part in range(2)]
    for copy in own_b:
        copy.start()

    def half(hh):
        return pl.ds(pl.multiple_of(rb * ((hh + t) % 2), 8), rb)

    my_planes = pl.ds(h * 2, 2)
    other = dev(q, 1 - h, t)
    c_copies = [
        remote(cond_hbm.at[:, :, half(1 - h), :], cond.at[pl.ds(0, DIM), my_planes], c_send.at[0], c_recv.at[0], other),
        remote(mean_hbm.at[:, half(1 - h), :], cond.at[DIM, my_planes], c_send.at[1], c_recv.at[1], other),
    ]
    own_c = [
        pltpu.make_async_copy(cond_hbm.at[:, :, half(h), :], cond.at[pl.ds(0, DIM), my_planes], local_sem.at[2]),
        pltpu.make_async_copy(mean_hbm.at[:, half(h), :], cond.at[DIM, my_planes], local_sem.at[3]),
    ]
    for copy in c_copies + own_c:
        copy.start()

    def clear(plane):
        def body(j, carry):
            zero = jnp.zeros((rb, 128), jnp.float32)
            bufb[j, plane, first:last, :] = zero
            bufd[j, plane, first:last, :] = zero
            return carry
        lax.fori_loop(0, terms, body, 0)

    @pl.when(q == 0)
    def _():
        clear(0)

    @pl.when(q == pairs - 1)
    def _():
        clear(5)

    def clear_rows(j, carry):
        zero = jnp.zeros((4, 1, 128), jnp.float32)
        for buf in (bufb, bufd):
            buf[j, 1:5, first - 1:first, :] = zero
            buf[j, 1:5, last:last + 1, :] = zero
        return carry

    lax.fori_loop(0, terms, clear_rows, 0)

    @pl.when(g == 0)
    def _():
        for step in range(2):
            rows_in[step, 0] = jnp.zeros(rows_in.shape[2:], jnp.float32)

    @pl.when(g == bands - 1)
    def _():
        for step in range(2):
            rows_in[step, 1] = jnp.zeros(rows_in.shape[2:], jnp.float32)

    def z_copy(step, buf, hh, part, at, size):
        slot = step * bands + hh * nt + part
        return remote(
            buf.at[pl.ds(at, size), 1 + 3 * hh, pl.ds(first, rb), :],
            buf.at[pl.ds(at, size), 5 * (1 - hh), pl.ds(first, rb), :],
            z_send.at[slot], z_recv.at[slot], dev(q - 1 + 2 * hh, h, t),
        )

    def z_sends(hh):
        target = q - 1 + 2 * hh
        return jnp.logical_and(target >= 0, target < pairs)

    def z_receives(hh):
        source = q + 1 - 2 * hh
        return jnp.logical_and(source >= 0, source < pairs)

    def forward(hh, tt):
        @pl.when(z_sends(hh))
        def _():
            z_copy(0, bufb, hh, tt, tt * tp, tp).start()

    def row_copies(step, part):
        up_h, up_t = owner(lax.rem(g + bands - 1, bands))
        down_h, down_t = owner(lax.rem(g + 1, bands))
        up = remote(
            rows_out.at[step, 0, part], rows_in.at[step, 1, part],
            r_send.at[step, 0, part], r_recv.at[step, 1, part], dev(q, up_h, up_t))
        down = remote(
            rows_out.at[step, 1, part], rows_in.at[step, 0, part],
            r_send.at[step, 1, part], r_recv.at[step, 0, part], dev(q, down_h, down_t))
        return up, down

    def planes_of(step, part):
        if step == 0:
            return ((0, 3), (1, 2))[part]
        return 2 * part, 2 * part + 1

    def send_rows(step, part, buf):
        planes = planes_of(step, part)

        def body(jt, carry):
            for tt in range(nt):
                for w in range(2):
                    at = 2 * tt + w
                    j = tt * tp + jt
                    rows_out[step, 0, part, jt, at:at + 1, :] = buf[j, planes[w] + 1, first:first + 1, :]
                    rows_out[step, 1, part, jt, at:at + 1, :] = buf[j, planes[w] + 1, last - 1:last, :]
            return carry
        lax.fori_loop(0, tp, body, 0)
        up, down = row_copies(step, part)

        @pl.when(g > 0)
        def _():
            up.start()

        @pl.when(g < bands - 1)
        def _():
            down.start()

    def wait_rows(step):
        for part in range(2):
            up, down = row_copies(step, part)

            @pl.when(g > 0)
            def _():
                down.wait_recv()

            @pl.when(g < bands - 1)
            def _():
                up.wait_recv()

    def end_rows(step):
        for part in range(2):
            up, down = row_copies(step, part)

            @pl.when(g > 0)
            def _():
                up.wait_send()

            @pl.when(g < bands - 1)
            def _():
                down.wait_send()

    def laplacian(buf):
        lane = lax.broadcasted_iota(jnp.int32, (4, rb, 128), 2)

        def body(jj, carry):
            for a in range(2):
                j = 2 * jj + a
                field = buf[j, 1:5, first:last, :]
                beside = buf[j, 2:6, first:last, :] + buf[j, 0:4, first:last, :]
                beside = beside + buf[j, 1:5, first + 1:last + 1, :] + buf[j, 1:5, first - 1:last - 1, :]
                after = jnp.where(lane == 127, 0.0, pltpu.roll(field, 127, 2))
                before = jnp.where(lane == 0, 0.0, pltpu.roll(field, 1, 2))
                lap[j] = 6.0 * field - (beside + after + before)
            return carry
        lax.fori_loop(0, terms // 2, body, 0)

    def correct(step):
        def body(jt, carry):
            for part in range(2):
                planes = planes_of(step, part)
                for tt in range(nt):
                    for w in range(2):
                        at = 2 * tt + w
                        j = tt * tp + jt
                        p = planes[w]
                        lap[j, p, 0:1, :] = lap[j, p, 0:1, :] - rows_in[step, 0, part, jt, at:at + 1, :]
                        lap[j, p, rb - 1:rb, :] = lap[j, p, rb - 1:rb, :] - rows_in[step, 1, part, jt, at:at + 1, :]
            return carry
        lax.fori_loop(0, tp, body, 0)

    table = galerkin_entries(DIM, DEG)

    def coupled(hh, finish):
        def body(w, carry):
            p = 2 * hh + w
            factors = [cond[k, p] for k in range(DIM)]
            mean = cond[DIM, p]
            for i in range(terms):
                total = mean * lap[i, p]
                for k in range(DIM):
                    mixed = None
                    for col, value in table[i][k]:
                        part = value * lap[col, p]
                        mixed = part if mixed is None else mixed + part
                    if mixed is not None:
                        total = total + factors[k] * mixed
                finish(i, p, total)
            return carry
        lax.fori_loop(0, 2, body, 0)

    center = 0.5 * (upper_edge + lower_edge)
    half_width = 0.5 * (upper_edge - lower_edge)
    sigma = center / half_width
    rho = 1.0 / sigma
    rho_next = 1.0 / (2.0 * sigma - rho)

    def finish_first(i, p, total):
        b = bufb[i, p + 1, first:last, :]
        residual = b - (1.0 / center) * total
        start = (1.0 / center) * b
        direction = (rho_next * rho) * start + (2.0 * rho_next / half_width) * residual
        r1[i, p] = residual
        bufd[i, p + 1, first:last, :] = direction
        sol[i, p] = start + direction

    def finish_second(i, p, total):
        r1[i, p] = r1[i, p] - total

    out_copies = []
    own_out = []

    def send_half(which, dh, src, dst):
        for n, (dh_n, dt) in enumerate(offsets):
            if dh_n == dh:
                hh, tt = partner(1, dh, dt)
                slot = which * len(offsets) + n
                copy = remote(
                    src.at[pl.ds(tt * tp, tp), pl.ds(hh * 2, 2)],
                    dst.at[:, :, band_rows(g), :],
                    o_send.at[slot], o_recv.at[slot], dev(q, hh, tt),
                )
                copy.start()
                out_copies.append(copy)
        if dh == 0:
            copy = pltpu.make_async_copy(
                src.at[pl.ds(t * tp, tp), pl.ds(h * 2, 2)], dst.at[:, :, band_rows(g), :], local_sem.at[4 + which])
            copy.start()
            own_out.append(copy)

    for part in range(2):
        own_b[part].wait()
        if part == 0:
            forward(h, t)
        for n, (dh, dt) in enumerate(offsets):
            b_copies[part * len(offsets) + n].wait_recv()
            if part == 0:
                hh, tt = partner(-1, dh, dt)
                forward(hh, tt)
        send_rows(0, part, bufb)
    for hh in range(2):
        @pl.when(z_receives(hh))
        def _(hh=hh):
            for tt in range(nt):
                z_copy(0, bufb, hh, tt, tt * tp, tp).wait_recv()
    laplacian(bufb)
    for copy in own_c:
        copy.wait()
    for copy in c_copies:
        copy.wait()
    wait_rows(0)
    correct(0)
    for dh in (1, 0):
        hh = (h + dh) % 2
        coupled(hh, finish_first)
        send_rows(1, hh, bufd)

        @pl.when(z_sends(hh))
        def _(hh=hh):
            z_copy(1, bufd, hh, 0, 0, terms).start()
        send_half(0, dh, sol, sol_hbm)

    for hh in range(2):
        @pl.when(z_receives(hh))
        def _(hh=hh):
            z_copy(1, bufd, hh, 0, 0, terms).wait_recv()
    laplacian(bufd)
    wait_rows(1)
    correct(1)
    for dh in (1, 0):
        coupled((h + dh) % 2, finish_second)
        send_half(1, dh, r1, res_hbm)

    for copy in b_copies:
        copy.wait_send()
    for step in range(2):
        end_rows(step)
    for hh in range(2):
        @pl.when(z_sends(hh))
        def _(hh=hh):
            for tt in range(nt):
                z_copy(0, bufb, hh, tt, tt * tp, tp).wait_send()
            z_copy(1, bufd, hh, 0, 0, terms).wait_send()
    for copy in own_out:
        copy.wait()
    for copy in out_copies:
        copy.wait()


def solution(mesh):
    slabs, nt = mesh.shape["slab"], mesh.shape["term"]

    def shards(right_side, mean_cond, cond_terms):
        tp, zp, ny, nx = right_side.shape
        assert zp == 2
        terms = tp * nt
        rb = ny // (2 * nt)
        partners = 2 * nt - 1
        return pl.pallas_call(
            functools.partial(kernel, (slabs, nt, tp, rb, terms)),
            out_shape=[jax.ShapeDtypeStruct(right_side.shape, jnp.float32)] * 2,
            in_specs=[pl.BlockSpec(memory_space=pltpu.HBM)] * 3,
            out_specs=[pl.BlockSpec(memory_space=pl.ANY)] * 2,
            scratch_shapes=[
                pltpu.VMEM((terms, 6, rb + 16, nx), jnp.float32),
                pltpu.VMEM((terms, 6, rb + 16, nx), jnp.float32),
                pltpu.VMEM((terms, 4, rb, nx), jnp.float32),
                pltpu.VMEM((terms, 4, rb, nx), jnp.float32),
                pltpu.VMEM((terms, 4, rb, nx), jnp.float32),
                pltpu.VMEM((DIM + 1, 4, rb, nx), jnp.float32),
                pltpu.VMEM((2, 2, 2, tp, 2 * nt, nx), jnp.float32),
                pltpu.VMEM((2, 2, 2, tp, 2 * nt, nx), jnp.float32),
                pltpu.SemaphoreType.DMA((6,)),
                pltpu.SemaphoreType.DMA((2 * partners,)),
                pltpu.SemaphoreType.DMA((2 * partners,)),
                pltpu.SemaphoreType.DMA((2,)),
                pltpu.SemaphoreType.DMA((2,)),
                pltpu.SemaphoreType.DMA((4 * nt,)),
                pltpu.SemaphoreType.DMA((4 * nt,)),
                pltpu.SemaphoreType.DMA((2, 2, 2)),
                pltpu.SemaphoreType.DMA((2, 2, 2)),
                pltpu.SemaphoreType.DMA((2 * partners,)),
                pltpu.SemaphoreType.DMA((2 * partners,)),
            ],
            compiler_params=pltpu.CompilerParams(
                collective_id=0, has_side_effects=True, vmem_limit_bytes=48 * 2**20
            ),
        )(right_side, mean_cond, cond_terms)

    placed = (P("term", "slab", None, None), P("slab", "term", None), P(None, "slab", "term", None))
    return jax.shard_map(
        shards,
        mesh=mesh,
        in_specs=placed,
        out_specs=(P("term", "slab", None, None), P("term", "slab", None, None)),
        check_vma=False,
    )
```

time: 120 us -> 116 us (0.967)
  Pallas kernels: 115 us -> 110 us
    pallas_call x1, Pallas kernels: 115 us -> 110 us  [shards(): pl.pallas_call(functools.partial(kernel, (slabs, nt, tp, rb, terms)), out...]
where the time goes in v2:
time: 116 us
  Pallas kernels  110 us (95%)
  local copies, waits for them, and re-layouts  4.75 us (4%)
    pallas_call x1, Pallas kernels, shards(): pl.pallas_call(functools.partial(kernel, (slabs, nt, tp, rb, terms)), out...  110 us
    unnamed x6, local copies, waits for them, and re-layouts  4.75 us

profile of v2, /device:TPU:0, one launch (start us, length us, event | category | flops | bytes accessed | tf_op | source)
XLA Modules:
  0.0 115.7 jit_solution(3687484930059368063)
XLA Ops:
  0.6 0.0 copy-start
  0.6 0.9 copy-done
  1.6 0.0 copy-start.1
  1.6 0.8 copy-done.1
  2.3 110.3 %shard_map.50 = (f32[21,2,128,128]{3,2,1,0:T(8,128)S(1)}, f32[21,2,128,128]{3,2,1,0:T(8,128)S(1)}) custom-call(f32[21,2,128,128]{3,2,1,0:T(8,128)} %b_hbm.1, f32[2,32,128]{2,1,0:T(8,128)S(1)} %copy-done.1, f32[6,2,32,128]{3,2,1,0:T(8,128)S(1)} %copy-done), custom_call_target="tpu_custom_call" | custom-call | tf_op jit(solution)/shard_map/pallas_call | solution.py:419
  112.6 1.5 %copy.7 = f32[21,2,128,128]{3,2,1,0:T(8,128)} copy(f32[21,2,128,128]{3,2,1,0:T(8,128)S(1)} %get-tuple-element.4) | data formatting | bytes 5505024
  114.1 1.5 %copy.8 = f32[21,2,128,128]{3,2,1,0:T(8,128)} copy(f32[21,2,128,128]{3,2,1,0:T(8,128)S(1)} %get-tuple-element.5) | data formatting | bytes 5505024
Async XLA Ops:
  0.6 0.9 copy-start
  1.6 0.8 copy-start.1

commit v3 on v2

--- a/solution.py
+++ b/solution.py
@@ -76,14 +76,21 @@
     def dev(qq, hh, tt):
         return {"slab": 2 * qq + hh, "term": tt}
 
-    offsets = [(dh, dt) for dh in (1, 0) for dt in range(nt - 1, -1, -1) if (dh, dt) != (0, 0)]
-
-    def partner(sign, dh, dt):
-        return (h + dh) % 2, (t + sign * dt + nt) % nt
+    u, c = t // 2, t % 2
+    offsets = [
+        (1 - c, c, 0), (c, 1 - c, 0), (1 - c, c, 1), (c, 1 - c, 1),
+        (1, 1, 0), (1, 1, 1), (0, 0, 1),
+    ]
+
+    def partner(dh, du, dc):
+        return (h + dh) % 2, 2 * ((u + du) % 2) + (c + dc) % 2
+
+    def slot_of(round_, dh, du, dc):
+        return len(offsets) * round_ + 4 * dh + 2 * du + dc - 1
 
     barrier = pltpu.get_barrier_semaphore()
-    for dh, dt in offsets:
-        hh, tt = partner(1, dh, dt)
+    for offset in offsets:
+        hh, tt = partner(*offset)
         pl.semaphore_signal(barrier, inc=1, device_id=dev(q, hh, tt), device_id_type=pl.DeviceIdType.MESH)
 
     @pl.when(q > 0)
@@ -115,10 +122,10 @@
 
     b_copies = []
     for part in range(2):
-        for n, (dh, dt) in enumerate(offsets):
-            hh, tt = partner(1, dh, dt)
+        for offset in offsets:
+            hh, tt = partner(*offset)
             src, dst = b_pair(part, band_of(hh, tt))
-            slot = part * len(offsets) + n
+            slot = slot_of(part, *offset)
             copy = remote(src, dst, b_send.at[slot], b_recv.at[slot], dev(q, hh, tt))
             copy.start()
             b_copies.append(copy)
@@ -260,18 +267,33 @@
             def _():
                 down.wait_send()
 
-    def laplacian(buf):
-        lane = lax.broadcasted_iota(jnp.int32, (4, rb, 128), 2)
-
+    lane = lax.broadcasted_iota(jnp.int32, (rb, 128), 1)
+
+    def lateral(buf, j, plane):
+        field = buf[j, plane, first:last, :]
+        beside = buf[j, plane, first + 1:last + 1, :] + buf[j, plane, first - 1:last - 1, :]
+        after = jnp.where(lane == 127, 0.0, pltpu.roll(field, 127, 1))
+        before = jnp.where(lane == 0, 0.0, pltpu.roll(field, 1, 1))
+        return 6.0 * field - (beside + after + before)
+
+    def laplacian_outer(buf):
         def body(jj, carry):
             for a in range(2):
                 j = 2 * jj + a
-                field = buf[j, 1:5, first:last, :]
-                beside = buf[j, 2:6, first:last, :] + buf[j, 0:4, first:last, :]
-                beside = beside + buf[j, 1:5, first + 1:last + 1, :] + buf[j, 1:5, first - 1:last - 1, :]
-                after = jnp.where(lane == 127, 0.0, pltpu.roll(field, 127, 2))
-                before = jnp.where(lane == 0, 0.0, pltpu.roll(field, 1, 2))
-                lap[j] = 6.0 * field - (beside + after + before)
+                lap[j, 0] = lateral(buf, j, 1)
+                lap[j, 3] = lateral(buf, j, 4)
+            return carry
+        lax.fori_loop(0, terms // 2, body, 0)
+
+    def laplacian_rest(buf):
+        def body(jj, carry):
+            for a in range(2):
+                j = 2 * jj + a
+                planes = [buf[j, p, first:last, :] for p in range(6)]
+                lap[j, 0] = lap[j, 0] - (planes[0] + planes[2])
+                lap[j, 1] = lateral(buf, j, 2) - (planes[1] + planes[3])
+                lap[j, 2] = lateral(buf, j, 3) - (planes[2] + planes[4])
+                lap[j, 3] = lap[j, 3] - (planes[3] + planes[5])
             return carry
         lax.fori_loop(0, terms // 2, body, 0)
 
@@ -330,40 +352,39 @@
     out_copies = []
     own_out = []
 
-    def send_half(which, dh, src, dst):
-        for n, (dh_n, dt) in enumerate(offsets):
-            if dh_n == dh:
-                hh, tt = partner(1, dh, dt)
-                slot = which * len(offsets) + n
-                copy = remote(
-                    src.at[pl.ds(tt * tp, tp), pl.ds(hh * 2, 2)],
-                    dst.at[:, :, band_rows(g), :],
-                    o_send.at[slot], o_recv.at[slot], dev(q, hh, tt),
-                )
-                copy.start()
-                out_copies.append(copy)
-        if dh == 0:
-            copy = pltpu.make_async_copy(
-                src.at[pl.ds(t * tp, tp), pl.ds(h * 2, 2)], dst.at[:, :, band_rows(g), :], local_sem.at[4 + which])
+    def send_out(which, src, dst):
+        for offset in offsets:
+            hh, tt = partner(*offset)
+            slot = slot_of(which, *offset)
+            copy = remote(
+                src.at[pl.ds(tt * tp, tp), pl.ds(hh * 2, 2)],
+                dst.at[:, :, band_rows(g), :],
+                o_send.at[slot], o_recv.at[slot], dev(q, hh, tt),
+            )
             copy.start()
-            own_out.append(copy)
+            out_copies.append(copy)
+        copy = pltpu.make_async_copy(
+            src.at[pl.ds(t * tp, tp), pl.ds(h * 2, 2)], dst.at[:, :, band_rows(g), :], local_sem.at[4 + which])
+        copy.start()
+        own_out.append(copy)
 
     for part in range(2):
         own_b[part].wait()
         if part == 0:
             forward(h, t)
-        for n, (dh, dt) in enumerate(offsets):
+        for n in [6, 0, 1, 2, 3, 4, 5]:
             b_copies[part * len(offsets) + n].wait_recv()
             if part == 0:
-                hh, tt = partner(-1, dh, dt)
-                forward(hh, tt)
+                forward(*partner(*offsets[n]))
         send_rows(0, part, bufb)
+        if part == 0:
+            laplacian_outer(bufb)
     for hh in range(2):
         @pl.when(z_receives(hh))
         def _(hh=hh):
             for tt in range(nt):
                 z_copy(0, bufb, hh, tt, tt * tp, tp).wait_recv()
-    laplacian(bufb)
+    laplacian_rest(bufb)
     for copy in own_c:
         copy.wait()
     for copy in c_copies:
@@ -378,18 +399,19 @@
         @pl.when(z_sends(hh))
         def _(hh=hh):
             z_copy(1, bufd, hh, 0, 0, terms).start()
-        send_half(0, dh, sol, sol_hbm)
+    send_out(0, sol, sol_hbm)
+    laplacian_outer(bufd)
 
     for hh in range(2):
         @pl.when(z_receives(hh))
         def _(hh=hh):
             z_copy(1, bufd, hh, 0, 0, terms).wait_recv()
-    laplacian(bufd)
+    laplacian_rest(bufd)
     wait_rows(1)
     correct(1)
     for dh in (1, 0):
         coupled((h + dh) % 2, finish_second)
-        send_half(1, dh, r1, res_hbm)
+    send_out(1, r1, res_hbm)
 
     for copy in b_copies:
         copy.wait_send()
@@ -412,7 +434,7 @@
 
     def shards(right_side, mean_cond, cond_terms):
         tp, zp, ny, nx = right_side.shape
-        assert zp == 2
+        assert zp == 2 and nt == 4
         terms = tp * nt
         rb = ny // (2 * nt)
         partners = 2 * nt - 1

time: 116 us -> 114 us (0.983)
  Pallas kernels: 110 us -> 108 us
    pallas_call x1, Pallas kernels: 110 us -> 108 us  [shards(): pl.pallas_call(functools.partial(kernel, (slabs, nt, tp, rb, terms)), out...]
where the time goes in v3:
time: 114 us; the launch traced here: 113 us
  Pallas kernels  108 us (95%)
  local copies, waits for them, and re-layouts  4.75 us (4%)
    pallas_call x1, Pallas kernels, shards(): pl.pallas_call(functools.partial(kernel, (slabs, nt, tp, rb, terms)), out...  108 us
    unnamed x6, local copies, waits for them, and re-layouts  4.75 us

profile of v3, /device:TPU:0, one launch (start us, length us, event | category | flops | bytes accessed | tf_op | source)
XLA Modules:
  0.0 113.2 jit_solution(10920894424213819136)
XLA Ops:
  0.6 0.0 copy-start
  0.6 0.9 copy-done
  1.6 0.0 copy-start.1
  1.6 0.8 copy-done.1
  2.3 107.8 %shard_map.50 = (f32[21,2,128,128]{3,2,1,0:T(8,128)S(1)}, f32[21,2,128,128]{3,2,1,0:T(8,128)S(1)}) custom-call(f32[21,2,128,128]{3,2,1,0:T(8,128)} %b_hbm.1, f32[2,32,128]{2,1,0:T(8,128)S(1)} %copy-done.1, f32[6,2,32,128]{3,2,1,0:T(8,128)S(1)} %copy-done), custom_call_target="tpu_custom_call" | custom-call | tf_op jit(solution)/shard_map/pallas_call | solution.py:441
  110.2 1.5 %copy.7 = f32[21,2,128,128]{3,2,1,0:T(8,128)} copy(f32[21,2,128,128]{3,2,1,0:T(8,128)S(1)} %get-tuple-element.4) | data formatting | bytes 5505024
  111.7 1.5 %copy.8 = f32[21,2,128,128]{3,2,1,0:T(8,128)} copy(f32[21,2,128,128]{3,2,1,0:T(8,128)S(1)} %get-tuple-element.5) | data formatting | bytes 5505024
Async XLA Ops:
  0.6 0.9 copy-start
  1.6 0.8 copy-start.1

commit v4 on v3

--- a/solution.py
+++ b/solution.py
@@ -352,8 +352,11 @@
     out_copies = []
     own_out = []
 
-    def send_out(which, src, dst):
-        for offset in offsets:
+    halves = ((h + 1 - c) % 2, (h + c) % 2)
+
+    def send_out(which, part, src, dst):
+        for n in ((0, 2), (1, 3, 4, 5, 6))[part]:
+            offset = offsets[n]
             hh, tt = partner(*offset)
             slot = slot_of(which, *offset)
             copy = remote(
@@ -363,10 +366,11 @@
             )
             copy.start()
             out_copies.append(copy)
-        copy = pltpu.make_async_copy(
-            src.at[pl.ds(t * tp, tp), pl.ds(h * 2, 2)], dst.at[:, :, band_rows(g), :], local_sem.at[4 + which])
-        copy.start()
-        own_out.append(copy)
+        if part == 1:
+            copy = pltpu.make_async_copy(
+                src.at[pl.ds(t * tp, tp), pl.ds(h * 2, 2)], dst.at[:, :, band_rows(g), :], local_sem.at[4 + which])
+            copy.start()
+            own_out.append(copy)
 
     for part in range(2):
         own_b[part].wait()
@@ -391,15 +395,14 @@
         copy.wait()
     wait_rows(0)
     correct(0)
-    for dh in (1, 0):
-        hh = (h + dh) % 2
+    for part, hh in enumerate(halves):
         coupled(hh, finish_first)
         send_rows(1, hh, bufd)
 
         @pl.when(z_sends(hh))
         def _(hh=hh):
             z_copy(1, bufd, hh, 0, 0, terms).start()
-    send_out(0, sol, sol_hbm)
+        send_out(0, part, sol, sol_hbm)
     laplacian_outer(bufd)
 
     for hh in range(2):
@@ -409,9 +412,9 @@
     laplacian_rest(bufd)
     wait_rows(1)
     correct(1)
-    for dh in (1, 0):
-        coupled((h + dh) % 2, finish_second)
-    send_out(1, r1, res_hbm)
+    for part, hh in enumerate(halves):
+        coupled(hh, finish_second)
+        send_out(1, part, r1, res_hbm)
 
     for copy in b_copies:
         copy.wait_send()
@@ -465,7 +468,7 @@
                 pltpu.SemaphoreType.DMA((2 * partners,)),
             ],
             compiler_params=pltpu.CompilerParams(
-                collective_id=0, has_side_effects=True, vmem_limit_bytes=48 * 2**20
+                collective_id=0, has_side_effects=True, vmem_limit_bytes=56 * 2**20
             ),
         )(right_side, mean_cond, cond_terms)
 

time: 114 us -> 114 us (level)
    unnamed x6 -> x4, local copies, waits for them, and re-layouts: 4.75 us -> 5.3 us
where the time goes in v4:
time: 114 us; the launch traced here: 113 us
  Pallas kernels  107 us (94%)
  local copies, waits for them, and re-layouts  5.3 us (5%)
    pallas_call x1, Pallas kernels, shards(): pl.pallas_call(functools.partial(kernel, (slabs, nt, tp, rb, terms)), out...  107 us
    unnamed x4, local copies, waits for them, and re-layouts  5.3 us

profile of v4, /device:TPU:0, one launch (start us, length us, event | category | flops | bytes accessed | tf_op | source)
XLA Modules:
  0.0 112.8 jit_solution(15981223402635583070)
XLA Ops:
  0.6 106.8 %shard_map.50 = (f32[21,2,128,128]{3,2,1,0:T(8,128)}, f32[21,2,128,128]{3,2,1,0:T(8,128)}) custom-call(f32[21,2,128,128]{3,2,1,0:T(8,128)} %b_hbm.1, f32[2,32,128]{2,1,0:T(8,128)} %mean_hbm.1, f32[6,2,32,128]{3,2,1,0:T(8,128)} %cond_hbm.1), custom_call_target="tpu_custom_call" | custom-call | tf_op jit(solution)/shard_map/pallas_call | solution.py:444
  107.4 0.0 copy-start
  107.5 3.8 %copy.7 = f32[21,2,128,128]{3,2,1,0:T(8,128)} copy(f32[21,2,128,128]{3,2,1,0:T(8,128)} %get-tuple-element.4) | data formatting | bytes 5505024
  111.2 0.0 copy-done
  111.2 1.5 %copy.8 = f32[21,2,128,128]{3,2,1,0:T(8,128)} copy(f32[21,2,128,128]{3,2,1,0:T(8,128)S(1)} %copy-done) | data formatting | bytes 5505024
Async XLA Ops:
  107.4 3.8 %copy-start = (f32[21,2,128,128]{3,2,1,0:T(8,128)S(1)}, f32[21,2,128,128]{3,2,1,0:T(8,128)}, u32[]{:S(2)}) copy-start(f32[21,2,128,128]{3,2,1,0:T(8,128)} %get-tuple-element.5) | copy-start | bytes 8257540
